TPU v7x, 32 devices: a whole 2x2x4 slice. The times are simulated.
32 devices in a mesh: parts: 2 (over x), band: 2 (over core), block: 8 (over z, y).
Axes of the slice: x: 2, y: 2, z: 4, core: 2. Of those that a mesh axis runs over, the one named last changes fastest.
Arguments:
- grid_input: bfloat16 [256, 128, 256], P(('parts', 'band'), 'block'), parts along dimension 0, may hold values from -6 to 6
- grad_output: bfloat16 [256, 128, 256], P(('parts', 'band'), 'block'), parts along dimension 0, may hold values from -6 to 6
- context_tile: int32 [64, 32], P(('parts', 'band'), 'block'), parts along dimension 0, may hold values from 0 to 127
- gains: float32 [2, 256], replicated, may hold values from 0.4 to 1.6
- row_weights: bfloat16 [4, 256, 256], replicated, may hold values from -0.375 to 0.375
- column_weights: bfloat16 [4, 256, 256], replicated, may hold values from -0.375 to 0.375
Outputs:
- grad_input: bfloat16 [256, 128, 256], P(('parts', 'band'), 'block'), parts along dimension 0
- grad_row_weights: float32 [8, 256, 256], P('parts'), parts along dimension 0
- grad_column_weights: float32 [8, 256, 256], P('parts'), parts along dimension 0
- grad_gains: float32 [4, 256], P('parts'), parts along dimension 0
- grad_context: float32 [256, 256], P(('parts', 'band', 'block')), parts along dimension 0
There are 2 independent parts, one for each index of `parts`. A program takes and returns all parts, laid end to end along the dimension named above; an argument that names none is the same for every part. Nothing has to cross between parts.
Inputs may be any that keep to these rules, and one draw needn't show every extreme that they name: `context_tile`: each patch reads one tile.
All inputs are finite; a program needn't handle non-finite values.
Results may differ from a plain program's by a relative error of at most 0.012.
The roundings to bfloat16 on the way count: a program that leaves them out, or rounds other values in their place, can miss the bound.
Values may be sent and summed in bfloat16 or wider, within the bound.
A program may use at most 64 MiB of HBM per device.

v0:
```python
import math

import jax
import jax.numpy as jnp
from jax import lax
from jax.sharding import PartitionSpec as P

HEADS = 8
TILE_DEV = 8


EPS = 1e-06


def project_in(inputs, gain, weights):
    features = inputs.shape[-1]
    widened = inputs.astype(jnp.float32)
    inverse_rms = lax.rsqrt(jnp.mean(widened * widened, axis=-1, keepdims=True) + EPS)
    unit_rows = widened * inverse_rms
    normed = (unit_rows * gain).astype(jnp.bfloat16)
    stacked = jnp.concatenate([weights[0], weights[1], weights[2]], axis=1)
    projected = jnp.dot(normed.reshape(-1, features), stacked, preferred_element_type=jnp.float32)
    packed = projected.astype(jnp.bfloat16).reshape(inputs.shape[:-1] + (3 * features,))
    return (normed, unit_rows, inverse_rms, packed)


def head_attend(queries, key_rows, values, direction):
    scaling = 1.0 / math.sqrt(queries.shape[-1])
    if direction == "row":
        scores = jnp.einsum("ald,amd->alm", queries, key_rows, preferred_element_type=jnp.float32)
    else:
        scores = jnp.einsum("lbd,mbd->blm", queries, key_rows, preferred_element_type=jnp.float32)
    soft_weights = jax.nn.softmax(scores * scaling, axis=-1).astype(jnp.bfloat16)
    if direction == "row":
        result = jnp.einsum(
            "alm,amd->ald", soft_weights, values, preferred_element_type=jnp.float32
        )
    else:
        result = jnp.einsum(
            "blm,mbd->lbd", soft_weights, values, preferred_element_type=jnp.float32
        )
    return result.astype(jnp.bfloat16)


def split_heads(packed, head_count):
    features = packed.shape[-1] // 3
    head_size = features // head_count
    portions = []
    for member in range(3):
        portion = packed[..., member * features : (member + 1) * features]
        portion = portion.reshape(packed.shape[:-1] + (head_count, head_size))
        portions.append(jnp.moveaxis(portion, -2, 0))
    return portions


def join_heads(stacked):
    rearranged = jnp.moveaxis(stacked, 0, -2)
    return rearranged.reshape(
        rearranged.shape[:-2] + (rearranged.shape[-2] * rearranged.shape[-1],)
    )


def attend(packed, head_count, direction):
    queries, key_rows, values = split_heads(packed, head_count)
    results = lax.map(
        lambda triple: head_attend(triple[0], triple[1], triple[2], direction),
        (queries, key_rows, values),
    )
    return join_heads(results)


def attend_back(packed, grad_mixed, head_count, direction):
    queries, key_rows, values = split_heads(packed, head_count)
    head_size = queries.shape[-1]
    cotangents = jnp.moveaxis(
        grad_mixed.reshape(grad_mixed.shape[:-1] + (head_count, head_size)), -2, 0
    )

    def single_head(quad):
        _, pullback = jax.vjp(
            lambda first, second, third: head_attend(first, second, third, direction),
            quad[0],
            quad[1],
            quad[2],
        )
        return pullback(quad[3])

    grad_query, grad_key, grad_value = lax.map(single_head, (queries, key_rows, values, cotangents))
    return jnp.concatenate(
        [join_heads(grad_query), join_heads(grad_key), join_heads(grad_value)], axis=-1
    )


def project_out(inputs, mixed, weight_out):
    features = inputs.shape[-1]
    added = jnp.dot(mixed.reshape(-1, features), weight_out, preferred_element_type=jnp.float32)
    return (inputs.astype(jnp.float32) + added.reshape(inputs.shape)).astype(jnp.bfloat16)


def output_back(mixed, grad_sum, weight_out):
    features = mixed.shape[-1]
    flat_grad = grad_sum.reshape(-1, features)
    grad_mixed = lax.dot_general(
        flat_grad, weight_out, (((1,), (1,)), ((), ())), preferred_element_type=jnp.float32
    )
    grad_weight = lax.dot_general(
        mixed.reshape(-1, features),
        flat_grad,
        (((0,), (0,)), ((), ())),
        preferred_element_type=jnp.float32,
    )
    return (grad_mixed.astype(jnp.bfloat16).reshape(mixed.shape), grad_weight)


def input_back(normed, unit_rows, inverse_rms, grad_packed, gain, weights, grad_sum):
    features = normed.shape[-1]
    stacked = jnp.concatenate([weights[0], weights[1], weights[2]], axis=1)
    flat_packed = grad_packed.reshape(-1, 3 * features)
    grad_normed = lax.dot_general(
        flat_packed, stacked, (((1,), (1,)), ((), ())), preferred_element_type=jnp.float32
    )
    grad_normed = grad_normed.reshape(normed.shape)
    grad_stacked = lax.dot_general(
        normed.reshape(-1, features),
        flat_packed,
        (((0,), (0,)), ((), ())),
        preferred_element_type=jnp.float32,
    )
    grad_gain = jnp.sum((unit_rows * grad_normed).reshape(-1, features), axis=0)
    grad_unit = grad_normed * gain
    inner = jnp.mean(grad_unit * unit_rows, axis=-1, keepdims=True)
    result = grad_sum.astype(jnp.float32) + inverse_rms * (grad_unit - unit_rows * inner)
    return (result.astype(jnp.bfloat16), grad_stacked, grad_gain)


def stack_grads(grad_stacked, grad_out):
    features = grad_out.shape[0]
    return jnp.stack(
        [
            grad_stacked[:, :features],
            grad_stacked[:, features : 2 * features],
            grad_stacked[:, 2 * features :],
            grad_out,
        ]
    )


def shards(grid_input, grad_output, context_tile, gains, row_weights, column_weights):
    band_rows, block_cols, features = grid_input.shape
    normed_one, unit_one, inverse_one, packed_one = project_in(grid_input, gains[0], row_weights)
    packed_row = lax.all_to_all(packed_one, "block", split_axis=0, concat_axis=1, tiled=True)
    mixed_row = attend(packed_row, HEADS, "row")
    mixed_one = lax.all_to_all(mixed_row, "block", split_axis=1, concat_axis=0, tiled=True)
    hidden = project_out(grid_input, mixed_one, row_weights[3])
    hidden_col, grad_col = (
        lax.all_to_all(hidden, "band", split_axis=1, concat_axis=0, tiled=True),
        lax.all_to_all(grad_output, "band", split_axis=1, concat_axis=0, tiled=True),
    )
    normed_two, unit_two, inverse_two, packed_two = project_in(hidden_col, gains[1], column_weights)
    mixed_two = attend(packed_two, HEADS, "col")
    grad_mixed_two, grad_out_two = output_back(mixed_two, grad_col, column_weights[3])
    grad_packed_two = attend_back(packed_two, grad_mixed_two, HEADS, "col")
    grad_hidden_col, grad_stack_two, grad_gain_two = input_back(
        normed_two, unit_two, inverse_two, grad_packed_two, gains[1], column_weights, grad_col
    )
    grad_hidden = lax.all_to_all(grad_hidden_col, "band", split_axis=0, concat_axis=1, tiled=True)
    grad_mixed_one, grad_out_one = output_back(mixed_one, grad_hidden, row_weights[3])
    grad_mixed_row = lax.all_to_all(
        grad_mixed_one, "block", split_axis=0, concat_axis=1, tiled=True
    )
    grad_packed_row = attend_back(packed_row, grad_mixed_row, HEADS, "row")
    grad_packed_one = lax.all_to_all(
        grad_packed_row, "block", split_axis=1, concat_axis=0, tiled=True
    )
    grad_input, grad_stack_one, grad_gain_one = input_back(
        normed_one, unit_one, inverse_one, grad_packed_one, gains[0], row_weights, grad_hidden
    )
    row_terms = stack_grads(grad_stack_one, grad_out_one)
    col_terms = stack_grads(grad_stack_two, grad_out_two)
    gain_terms = jnp.stack([grad_gain_one, grad_gain_two])
    row_total, col_total, gain_total = lax.psum(
        (row_terms, col_terms, gain_terms), ("band", "block")
    )
    cell_count = band_rows * lax.axis_size("band") * block_cols * lax.axis_size("block")
    scaling = 1.0 / math.sqrt(cell_count)
    cell_grads = grad_input.reshape(-1, features)
    cell_tiles = jnp.repeat(jnp.repeat(context_tile, 4, axis=0), 4, axis=1).reshape(-1)
    own_rows = TILE_DEV
    columns = lax.iota(jnp.int32, own_rows * lax.axis_size(("band", "block")))
    onehot = (cell_tiles[:, None] == columns[None, :]).astype(jnp.bfloat16)
    summed = lax.dot_general(
        onehot, cell_grads, (((0,), (0,)), ((), ())), preferred_element_type=jnp.float32
    )
    every_tile = lax.psum(0.25 * summed, ("band", "block"))
    grad_context = lax.dynamic_slice_in_dim(
        every_tile, lax.axis_index(("band", "block")) * own_rows, own_rows, 0
    )
    return (
        grad_input,
        row_total * scaling,
        col_total * scaling,
        gain_total * scaling,
        grad_context,
    )


def solution(mesh):
    in_specs = (
        P(("parts", "band"), "block", None),
        P(("parts", "band"), "block", None),
        P(("parts", "band"), "block"),
        P(),
        P(),
        P(),
    )
    out_specs = (
        P(("parts", "band"), "block", None),
        P("parts", None, None),
        P("parts", None, None),
        P("parts", None),
        P(("parts", "band", "block"), None),
    )
    return jax.shard_map(shards, mesh=mesh, in_specs=in_specs, out_specs=out_specs, check_vma=False)
```

profile of v0, /device:TPU:0, one launch (start us, length us, event | category | flops | bytes accessed | tf_op | source)
XLA Modules:
  0.0 478.5 jit_solution(12935251995971966002)
XLA Ops:
  13.0 7.4 %all-to-all-start.1 = ((bf16[64,16,768]{2,1,0:T(8,128)(2,1)}), bf16[64,16,768]{2,1,0:T(8,128)(2,1)S(1)}, u32[]{:S(2)}, u32[]{:S(2)}) async-start(bf16[64,16,768]{2,1,0:T(8,128)(2,1)} %bitcast.488), calls=%async_computation.1 | async-start | bytes 3145728 | tf_op jit(solution)/shard_map/all_to_all | solution.py:151
  21.3 36.0 %all-to-all-done.1 = bf16[64,16,768]{2,1,0:T(8,128)(2,1)S(1)} async-done(((bf16[64,16,768]{2,1,0:T(8,128)(2,1)}), bf16[64,16,768]{2,1,0:T(8,128)(2,1)S(1)}, u32[]{:S(2)}, u32[]{:S(2)}) %all-to-all-start.1) | async-done | bytes 1572896 | tf_op jit(solution)/shard_map/all_to_all | solution.py:151
  57.4 3.5 all-to-all-start
  65.7 20.9 %while.48 = (s32[]{:T(128)}, bf16[8,8,128,32]{2,3,0,1:T(8,128)(2,1)S(1)}, bf16[8,8,128,32]{2,3,1,0:T(8,128)(2,1)}, bf16[8,8,128,32]{2,3,1,0:T(8,128)(2,1)}, bf16[8,8,128,32]{2,3,1,0:T(8,128)(2,1)S(1)}, /*index=5*/s32[]{:T(128)}) while((s32[]{:T(128)}, bf16[8,8,128,32]{2,3,0,1:T(8,128)(2,1)S(1)}, bf16[8,8,128,32]{2,3,1,0:T(8,128)(2,1)}, ...), condition=%wide.region_4.5_spmd, body=%wide.region_1.4_spmd.sunk | while | flops 26117376 | bytes 404549 | solution.py:65
  87.8 4.1 all-to-all-start.2
  95.2 2.6 reshape_reshape.6
  97.8 2.8 copy.300
  103.4 4.1 all-to-all-done.2
  110.1 4.2 all_to_all.102
  128.4 76.2 %while.49 = (s32[]{:T(128)}, bf16[8,128,8,32]{1,3,0,2:T(8,128)(2,1)}, bf16[8,128,8,32]{1,3,0,2:T(8,128)(2,1)}, bf16[8,128,8,32]{1,3,0,2:T(8,128)(2,1)}, bf16[8,1...) while((s32[]{:T(128)}, ...), condition=%wide.region_10.11_spmd, body=%wide.region_6.10_spmd.sunk | while | flops 70358528 | bytes 5300317 | solution.py:88
  210.9 2.9 multiply_reduce_fusion.2
  214.5 4.2 all_to_all.103
  222.3 3.6 all-to-all-start.5
  226.3 14.5 %all-to-all-done.5 = bf16[64,16,256]{2,1,0:T(8,128)(2,1)S(1)} async-done(((bf16[64,16,256]{2,1,0:T(8,128)(2,1)}), bf16[64,16,256]{2,1,0:T(8,128)(2,1)S(1)}, u32[]{:S(2)}, u32[]{:S(2)}) %all-to-all-start.5) | async-done | bytes 524320 | tf_op jit(solution)/shard_map/all_to_all | solution.py:168
  241.6 2.6 reshape.215
  244.3 2.2 copy.314
  247.5 66.1 %while.50 = (s32[]{:T(128)}, bf16[8,8,128,32]{2,3,0,1:T(8,128)(2,1)S(1)}, bf16[8,8,128,32]{2,3,0,1:T(8,128)(2,1)S(1)}, bf16[8,8,128,32]{2,3,0,1:T(8,128)(2,1)}, ...) while((s32[]{:T(128)}, ...), condition=%wide.region_16.17_spmd, body=%wide.region_12.0_spmd.sunk | while | flops 70358528 | bytes 5300317 | solution.py:88
  317.6 4.5 all-to-all-start.6
  322.2 26.0 %while.51 = (s32[]{:T(128)}, bf16[8,128,8,32]{1,3,2,0:T(8,128)(2,1)}, bf16[8,128,8,32]{1,3,2,0:T(8,128)(2,1)}, bf16[8,128,8,32]{1,3,2,0:T(8,128)(2,1)}, bf16[8,128,8,32]{1,3,2,0:T(8,128)(2,1)}, /*index=5*/s32[]{:T(128)}) while((s32[]{:T(128)}, bf16[8,128,8,32]{1,3,2,0:T(8,128)(2,1)}, bf16[8,128,8,32]{1,3,2,0:T(8,128)(2,1)}, ...), condition=%wide.region_22.23_spmd, body=%wide.region_19.22_spmd.sunk | while | flops 26117376 | bytes 404549 | solution.py:65
  348.2 3.9 copy.332
  352.1 2.2 reshape_reshape.7
  367.2 33.0 %psum.30 = f32[2,256]{1,0:T(2,128)S(1)} all-reduce(f32[2,256]{1,0:T(2,128)S(1)} %pad_maximum_fusion.12), channel_id=1, replica_groups=mesh['parts'=2,'band'=2,'block'=8] {'band','block'}, use_global_device_ids=true, to_apply=%region_26.27 | all-reduce | flops 512 | bytes 4096 | tf_op jit(solution)/shard_map/psum | solution.py:181
  400.8 66.6 %all-reduce.3.cloned.1.call-done = (f32[4,256,256]{2,1,0:T(8,128)}, f32[4,256,256]{2,1,0:T(8,128)}, f32[128,256]{1,0:T(8,128)}) async-done(((f32[4,256,256]{2,1,0:T(8,128)}, f32[4,256,256]{2,1,0:T(8,128)}, f32[128,256]{1,0:T(8,128)}), (f32[4,256,256]{2,1,0:T(8,128)}, f32[4,256,256]{2,1,0:T(8,128)}, f32[128,256]{1,0:T(8,128)})) %all-reduce.3.cloned.1.call-update) | async-done | bytes 2228240 | tf_op jit(solution)/shard_map/psum | solution.py:181
  467.3 3.1 broadcast_multiply_fusion
  (304 shorter events, 255.4 us)
Async XLA Ops:
  7.2 3.8 copy-start
  8.5 4.5 copy-start.23
  9.9 3.0 copy-start.19
  13.0 7.4 %copy-start.15 = (bf16[64,16,256]{2,1,0:T(8,128)(2,1)S(1)}, bf16[64,16,256]{2,1,0:T(8,128)(2,1)}, u32[]{:S(2)}) copy-start(bf16[64,16,256]{2,1,0:T(8,128)(2,1)} %param.15) | copy-start | bytes 1572868
  13.0 44.4 %all-to-all-start.1 = ((bf16[64,16,768]{2,1,0:T(8,128)(2,1)}), bf16[64,16,768]{2,1,0:T(8,128)(2,1)S(1)}, u32[]{:S(2)}, u32[]{:S(2)}) async-start(bf16[64,16,768]{2,1,0:T(8,128)(2,1)} %bitcast.488), calls=%async_computation.1 | async-start | bytes 3145728 | tf_op jit(solution)/shard_map/all_to_all | solution.py:151
  57.4 30.4 %all-to-all-start = ((bf16[64,16,256]{2,0,1:T(8,128)(2,1)}), bf16[64,16,256]{2,0,1:T(8,128)(2,1)S(1)}, u32[]{:S(2)}, u32[]{:S(2)}) async-start(bf16[64,16,256]{2,0,1:T(8,128)(2,1)} %copy.274), calls=%async_computation | async-start | bytes 1048576 | tf_op jit(solution)/shard_map/all_to_all | solution.py:157
  86.6 5.7 %copy-start.12 = (bf16[8,8,128,32]{2,3,1,0:T(8,128)(2,1)}, bf16[8,8,128,32]{2,3,1,0:T(8,128)(2,1)S(1)}, u32[]{:S(2)}) copy-start(bf16[8,8,128,32]{2,3,1,0:T(8,128)(2,1)S(1)} %get-tuple-element.661) | copy-start | bytes 1572868
  87.8 4.5 copy-start.3
  87.8 19.6 %all-to-all-start.2 = ((bf16[8,128,256]{2,0,1:T(8,128)(2,1)}), bf16[8,128,256]{2,0,1:T(8,128)(2,1)}, u32[]{:S(2)}, u32[]{:S(2)}) async-start(bf16[8,128,256]{2,0,1:T(8,128)(2,1)} %copy.287), calls=%async_computation.2 | async-start | bytes 1048576 | tf_op jit(solution)/shard_map/all_to_all | solution.py:153
  100.6 2.0 copy-start.14
  108.6 5.7 %copy-start.5 = (bf16[8,8,16,256]{3,2,1,0:T(8,128)(2,1)}, bf16[8,8,16,256]{3,2,1,0:T(8,128)(2,1)S(1)}, u32[]{:S(2)}) copy-start(bf16[8,8,16,256]{3,2,1,0:T(8,128)(2,1)S(1)} %copy.289) | copy-start | bytes 1572868
  204.5 6.4 %copy-start.9 = (f32[2,64,8,256]{3,1,0,2:T(8,128)S(1)}, f32[2,64,8,256]{3,1,0,2:T(8,128)}, u32[]{:S(2)}) copy-start(f32[2,64,8,256]{3,1,0,2:T(8,128)} %copy.310) | copy-start | bytes 3145732
  204.5 6.4 %copy-start.25 = (f32[1,256]{1,0:T(1,128)S(1)}, f32[1,256]{1,0:T(1,128)}, u32[]{:S(2)}) copy-start(f32[1,256]{1,0:T(1,128)} %get-tuple-element.371) | copy-start | bytes 3076
  219.4 6.5 %copy-start.26 = (s32[16,4]{0,1:T(4,128)S(1)}, s32[16,4]{0,1:T(4,128)}, u32[]{:S(2)}) copy-start(s32[16,4]{0,1:T(4,128)} %param.16) | copy-start | bytes 772
  222.3 18.5 %all-to-all-start.5 = ((bf16[64,16,256]{2,1,0:T(8,128)(2,1)}), bf16[64,16,256]{2,1,0:T(8,128)(2,1)S(1)}, u32[]{:S(2)}, u32[]{:S(2)}) async-start(bf16[64,16,256]{2,1,0:T(8,128)(2,1)} %bitcast.89), calls=%async_computation.5 | async-start | bytes 1048576 | tf_op jit(solution)/shard_map/all_to_all | solution.py:168
  317.6 42.2 %all-to-all-start.6 = ((bf16[8,128,768]{2,0,1:T(8,128)(2,1)}), bf16[8,128,768]{2,0,1:T(8,128)(2,1)}, u32[]{:S(2)}, u32[]{:S(2)}) async-start(bf16[8,128,768]{2,0,1:T(8,128)(2,1)} %copy.321), calls=%async_computation.6 | async-start | bytes 3145728 | tf_op jit(solution)/shard_map/all_to_all | solution.py:172
  322.2 145.2 %all-reduce.3.cloned.1.call-start = ((), (), s32[]{:S(2)}) async-start(), calls=%async_computation.7 | async-start | bytes 4456448 | tf_op jit(solution)/shard_map/psum | solution.py:181
  358.0 1.5 copy-start.8
  359.8 1.8 copy-start.20
  359.8 1.8 copy-start.24
  362.9 1.5 copy-start.2
  362.9 1.6 copy-start.21
  364.5 1.6 copy-start.13
  364.9 2.2 copy-start.10
  (9 other events, 8.7 us)
Sparse Core Ops, SparseCore 0:
  367.2 100.0 all-reduce.2
where the time goes:
time: 486 us; the launch traced here: 479 us
  matrix products  206 us (42%)
  waiting for transfers between devices  121 us (25%)
  local copies, waits for them, and re-layouts  58.4 us (12%)
  blocking collectives  41.4 us (9%)
  starting transfers between devices  23.2 us (5%)
  between operations  14.6 us (3%)
  other arithmetic  13.1 us (3%)
    psum x1, waiting for transfers between devices, shards(): lax.psum((row_terms, col_terms, gain_terms), ('band', 'block'))  66.6 us
    dot_general x24, matrix products, head_attend(): jnp.einsum('lbd,mbd->blm', queries, key_rows, preferred_element_type=jnp....  42.4 us
    sub x32, matrix products, head_attend(): jax.nn.softmax(scores * scaling, axis=-1).astype(jnp.bfloat16)  39.7 us
    dot_general x24, matrix products, head_attend(): jnp.einsum('blm,mbd->lbd', soft_weights, values, preferred_element_type=j...  39.6 us
    all_to_all x1, waiting for transfers between devices, shards(): lax.all_to_all(packed_one, 'block', split_axis=0, concat_axis=1, tiled=True)  36 us
    dot_general x24, matrix products, head_attend(): jnp.einsum('alm,amd->ald', soft_weights, values, preferred_element_type=j...  34.3 us
    psum x1, blocking collectives, shards(): lax.psum((row_terms, col_terms, gain_terms), ('band', 'block'))  33 us
    dot_general x24, matrix products, head_attend(): jnp.einsum('ald,amd->alm', queries, key_rows, preferred_element_type=jnp....  32.3 us
  transfers between devices with their start and end apart: 6, of which 4 were waited for; matrix products, arithmetic and copies ran while one was open for 16% of the time, Pallas kernels for 0%

commit v1 on v0

--- a/solution.py
+++ b/solution.py
@@ -1,8 +1,11 @@
+import functools
 import math
 
 import jax
 import jax.numpy as jnp
 from jax import lax
+from jax.experimental import pallas as pl
+from jax.experimental.pallas import tpu as pltpu
 from jax.sharding import PartitionSpec as P
 
 HEADS = 8
@@ -204,6 +207,480 @@
     )
 
 
+F32 = jnp.float32
+BF16 = jnp.bfloat16
+D = 256
+L = 128
+HD = D // HEADS
+SCALE = 1.0 / math.sqrt(HD)
+NB = 8
+ND = 2 * NB
+GROUP = 2
+CT = TILE_DEV * ND
+
+
+def fits_fused(mesh):
+    return mesh.shape["band"] == 2 and mesh.shape["block"] == NB
+
+
+def dot_nn(a, b):
+    return lax.dot_general(a, b, (((1,), (0,)), ((), ())), preferred_element_type=F32)
+
+
+def dot_nt(a, b):
+    return lax.dot_general(a, b, (((1,), (1,)), ((), ())), preferred_element_type=F32)
+
+
+def dot_tn(a, b):
+    return lax.dot_general(a, b, (((0,), (0,)), ((), ())), preferred_element_type=F32)
+
+
+def head_stack(a):
+    lane = lax.broadcasted_iota(jnp.int32, (1, D), 1)
+    wide = a.astype(F32)
+    return jnp.concatenate(
+        [jnp.where(lane // HD == h, wide, 0.0).astype(BF16) for h in range(HEADS)], axis=0
+    )
+
+
+def side_by_side(a):
+    return jnp.concatenate([a[h * L : (h + 1) * L] for h in range(HEADS)], axis=1)
+
+
+def norm_parts(v):
+    inverse = lax.rsqrt(jnp.mean(v * v, axis=-1, keepdims=True) + EPS)
+    return v * inverse, inverse
+
+
+def attn_probs(q, k):
+    s = dot_nt(head_stack(k), q) * SCALE
+    parts = []
+    for h in range(HEADS):
+        one = s[h * L : (h + 1) * L]
+        e = jnp.exp(one - jnp.max(one, axis=0, keepdims=True))
+        parts.append((e * (1.0 / jnp.sum(e, axis=0, keepdims=True))).astype(BF16))
+    return jnp.concatenate(parts, axis=0)
+
+
+def attn_out(p, v):
+    return dot_tn(p, head_stack(v)).astype(BF16)
+
+
+def attn_back(p, q, k, v, do):
+    dp = dot_nt(head_stack(v), do)
+    parts = []
+    for h in range(HEADS):
+        w = p[h * L : (h + 1) * L].astype(F32)
+        t = dp[h * L : (h + 1) * L]
+        t = t - jnp.sum(t * w, axis=0, keepdims=True)
+        parts.append((t * w * SCALE).astype(BF16))
+    ds = jnp.concatenate(parts, axis=0)
+    dq = dot_tn(ds, head_stack(k)).astype(BF16)
+    dk = dot_nn(side_by_side(ds), head_stack(q)).astype(BF16)
+    dv = dot_nn(side_by_side(p), head_stack(do)).astype(BF16)
+    return jnp.concatenate([dq, dk, dv], axis=1)
+
+
+def norm_back(v, c, dn, gain):
+    u, inverse = norm_parts(v)
+    du = dn * gain
+    inner = jnp.mean(du * u, axis=-1, keepdims=True)
+    dv = c + inverse * (du - u * inner)
+    return dv, jnp.sum(u * dn, axis=0, keepdims=True)
+
+
+def fused_kernel(
+    scaling,
+    x_ref, g_ref, ct_ref, gains_ref, wr_ref, wro_ref, wc_ref, wco_ref,
+    gi_ref, gr_ref, gc_ref, gg_ref, ctx_ref,
+    xbuf, ctin, flat, gsend, gcol, hsend, hrecv, cols, cots, ghsend, ghrecv,
+    nbuf, obuf, qkvbuf, pbuf, dbuf, cbuf, gisend,
+    wsend, wrecv, wfull, ctacc, ctrecv, gacc, grecv,
+    send_sem, recv_sem,
+):
+    band, block = lax.axis_index("band"), lax.axis_index("block")
+    me = band * NB + block
+    mycol = 2 * block + band
+
+    def peer(i):
+        other = lax.rem(me + i, ND)
+        return other, other // NB, lax.rem(other, NB)
+
+    def remote(phase, src, dst, to, frm, b, k):
+        return pltpu.make_async_remote_copy(
+            src_ref=src, dst_ref=dst, send_sem=send_sem.at[phase, to],
+            recv_sem=recv_sem.at[phase, frm],
+            device_id={"band": b, "block": k}, device_id_type=pl.DeviceIdType.MESH,
+        )
+
+    def every(fn, count):
+        def step(i, _):
+            fn(i)
+            return 0
+        lax.fori_loop(1, count, step, 0)
+
+    def rows64(ref, j):
+        return ref.at[pl.ds(pl.multiple_of(j * 64, 64), 64)]
+
+    def rows8(ref, j):
+        return ref.at[pl.ds(pl.multiple_of(j * 8, 8), 8)]
+
+    barrier = pltpu.get_barrier_semaphore()
+
+    def greet(i):
+        _, b, k = peer(i)
+        pl.semaphore_signal(
+            barrier, inc=1, device_id={"band": b, "block": k},
+            device_id_type=pl.DeviceIdType.MESH,
+        )
+
+    every(greet, ND)
+    pl.semaphore_wait(barrier, ND - 1)
+
+    def in_copy(to, frm):
+        return remote(
+            0, x_ref.at[pl.ds(pl.multiple_of(to * 8, 8), 8)],
+            xbuf.at[:, pl.ds(pl.multiple_of(frm * 16, 16), 16)], to, frm, band, to,
+        )
+
+    def ct_copy(to, frm):
+        return remote(1, ct_ref.at[to], ctin.at[frm], to, frm, band, to)
+
+    def ring(i):
+        return lax.rem(block + i, NB)
+
+    every(lambda i: in_copy(ring(i), block).start(), NB)
+    every(lambda i: ct_copy(ring(i), block).start(), NB)
+    xbuf[:, pl.ds(pl.multiple_of(block * 16, 16), 16)] = x_ref[pl.ds(pl.multiple_of(block * 8, 8), 8)]
+    ctin[block] = ct_ref[block]
+
+    def spread(t, _):
+        wide = g_ref[t].astype(F32)
+        base = (t // 8) * 64 + lax.rem(t, 8)
+        for half in range(2):
+            for lo in range(2):
+                flat[lo, pl.ds(base + half * 512, 8, stride=8), :] = wide[
+                    half * 8 : half * 8 + 8, lo * L : lo * L + L
+                ]
+        return 0
+
+    lax.fori_loop(0, 64, spread, 0)
+    for lo in range(2):
+        gsend[:, lo * L : lo * L + L] = flat[lo].astype(BF16)
+
+    def half512(ref, j):
+        return ref.at[pl.ds(pl.multiple_of(j * 512, 512), 512)]
+
+    def g_copy(to, frm):
+        return remote(2, half512(gsend, to), half512(gcol, frm), to, frm, to, block)
+
+    other = 1 - band
+    g_copy(other, band).start()
+    gcol[pl.ds(pl.multiple_of(band * 512, 512), 512)] = gsend[pl.ds(pl.multiple_of(band * 512, 512), 512)]
+
+    every(lambda i: in_copy(block, ring(i)).wait_recv(), NB)
+
+    gain_r = gains_ref[0:1, :]
+    gain_c = gains_ref[1:2, :]
+    span = GROUP * L
+
+    def row_fwd(t, _):
+        at = pl.ds(pl.multiple_of(t * span, span), span)
+        v = jnp.concatenate([xbuf[t * GROUP + i] for i in range(GROUP)], axis=0).astype(F32)
+        u, _inv = norm_parts(v)
+        n = (u * gain_r).astype(BF16)
+        qkv = dot_nn(n, wr_ref[...]).astype(BF16)
+        outs = []
+        for i in range(GROUP):
+            own = qkv[i * L : (i + 1) * L]
+            p = attn_probs(own[:, :D], own[:, D : 2 * D])
+            pbuf[t * GROUP + i] = p
+            outs.append(attn_out(p, own[:, 2 * D :]))
+        o = jnp.concatenate(outs, axis=0)
+        nbuf[at] = n
+        obuf[at] = o
+        qkvbuf[at] = qkv
+        hidden = v + dot_nn(o, wro_ref[...])
+        for i in range(GROUP):
+            for lo in range(2):
+                flat[lo, pl.ds(t * GROUP + i, L, stride=8), :] = hidden[
+                    i * L : (i + 1) * L, lo * L : lo * L + L
+                ]
+        return 0
+
+    lax.fori_loop(0, 8 // GROUP, row_fwd, 0)
+    for lo in range(2):
+        hsend[:, lo * L : lo * L + L] = flat[lo].astype(BF16)
+
+    def h_send(i):
+        o_, b, k = peer(i)
+        return remote(3, rows64(hsend, 2 * k + b), rows64(hrecv, me), o_, me, b, k)
+
+    def h_recv(i):
+        o_, b, k = peer(i)
+        return remote(3, rows64(hsend, mycol), rows64(hrecv, o_), o_, o_, b, k)
+
+    every(lambda i: h_send(i).start(), ND)
+    hrecv[pl.ds(pl.multiple_of(me * 64, 64), 64)] = hsend[pl.ds(pl.multiple_of(mycol * 64, 64), 64)]
+    g_copy(band, other).wait_recv()
+    cots[...] = gcol[...].astype(F32).reshape(ND, 8, 8, D)
+    every(lambda i: h_recv(i).wait_recv(), ND)
+    cols[...] = hrecv[...].astype(F32).reshape(ND, 8, 8, D)
+
+    gacc[...] = jnp.zeros_like(gacc)
+
+    def col_step(t, _):
+        at = pl.ds(pl.multiple_of(1024 + t * span, span), span)
+        v = jnp.concatenate([cols[:, t * GROUP + i].reshape(L, D) for i in range(GROUP)], axis=0)
+        c = jnp.concatenate([cots[:, t * GROUP + i].reshape(L, D) for i in range(GROUP)], axis=0)
+        cb = c.astype(BF16)
+        u, _inv = norm_parts(v)
+        n = (u * gain_c).astype(BF16)
+        qkv = dot_nn(n, wc_ref[...]).astype(BF16)
+        do = dot_nt(cb, wco_ref[...]).astype(BF16)
+        outs, backs = [], []
+        for i in range(GROUP):
+            own = qkv[i * L : (i + 1) * L]
+            q, k, w = own[:, :D], own[:, D : 2 * D], own[:, 2 * D :]
+            p = attn_probs(q, k)
+            outs.append(attn_out(p, w))
+            backs.append(attn_back(p, q, k, w, do[i * L : (i + 1) * L]))
+        dqkv = jnp.concatenate(backs, axis=0)
+        nbuf[at] = n
+        obuf[at] = jnp.concatenate(outs, axis=0)
+        dbuf[at] = dqkv
+        cbuf[at] = cb
+        dn = dot_nt(dqkv, wc_ref[...])
+        dv, ggain = norm_back(v, c, dn, gain_c)
+        gacc[1:2, :] += ggain
+        for i in range(GROUP):
+            cols[:, t * GROUP + i] = dv[i * L : (i + 1) * L].reshape(ND, 8, D)
+        return 0
+
+    lax.fori_loop(0, 8 // GROUP, col_step, 0)
+    ghsend[...] = cols[...].reshape(1024, D).astype(BF16)
+
+    def gh_send(i):
+        o_, b, k = peer(i)
+        return remote(4, rows64(ghsend, o_), rows64(ghrecv, mycol), o_, me, b, k)
+
+    def gh_recv(i):
+        o_, b, k = peer(i)
+        return remote(4, rows64(ghsend, me), rows64(ghrecv, 2 * k + b), o_, o_, b, k)
+
+    every(lambda i: gh_send(i).start(), ND)
+    ghrecv[pl.ds(pl.multiple_of(mycol * 64, 64), 64)] = ghsend[pl.ds(pl.multiple_of(me * 64, 64), 64)]
+
+    def weight_grads(start, slot):
+        span_all = pl.ds(start, 1024)
+        n = nbuf[span_all]
+        for m in range(3):
+            wsend[slot, m * D : (m + 1) * D] = (
+                dot_tn(n, dbuf[span_all, m * D : (m + 1) * D]) * scaling
+            ).astype(BF16)
+        wsend[slot, 3 * D : 4 * D] = (dot_tn(obuf[span_all], cbuf[span_all]) * scaling).astype(BF16)
+
+    def rs_send(slot, i):
+        o_, b, k = peer(i)
+        return remote(5 + slot, rows64(wsend.at[slot], o_), wrecv.at[slot, me], o_, me, b, k)
+
+    def rs_recv(slot, i):
+        o_, b, k = peer(i)
+        return remote(5 + slot, rows64(wsend.at[slot], me), wrecv.at[slot, o_], o_, o_, b, k)
+
+    def ag_send(slot, i):
+        o_, b, k = peer(i)
+        return remote(7 + slot, rows64(wfull.at[slot], me), rows64(wfull.at[slot], me), o_, me, b, k)
+
+    def ag_recv(slot, i):
+        o_, b, k = peer(i)
+        return remote(7 + slot, rows64(wfull.at[slot], me), rows64(wfull.at[slot], o_), o_, o_, b, k)
+
+    def reduce_own(slot):
+        every(lambda i: rs_recv(slot, i).wait_recv(), ND)
+        wrecv[slot, me] = wsend[slot, pl.ds(pl.multiple_of(me * 64, 64), 64)]
+        total = wrecv[slot, 0].astype(F32)
+        for j in range(1, ND):
+            total = total + wrecv[slot, j].astype(F32)
+        wfull[slot, pl.ds(pl.multiple_of(me * 64, 64), 64)] = total.astype(BF16)
+        every(lambda i: ag_send(slot, i).start(), ND)
+
+    weight_grads(1024, 1)
+    every(lambda i: rs_send(1, i).start(), ND)
+
+    every(lambda i: ct_copy(block, ring(i)).wait_recv(), NB)
+    tiles = ctin[0]
+    for j in range(1, NB):
+        tiles = tiles + ctin[j]
+    tile_ids = tiles.astype(jnp.int32)
+    ctin[0] = tile_ids.astype(F32)
+
+    every(lambda i: gh_recv(i).wait_recv(), ND)
+    for lo in range(2):
+        flat[lo] = ghrecv[:, lo * L : lo * L + L].astype(F32)
+
+    ctacc[...] = jnp.zeros_like(ctacc)
+
+    def gi_copy(to, frm):
+        return remote(
+            9, gisend.at[:, pl.ds(pl.multiple_of(to * 16, 16), 16)],
+            gi_ref.at[pl.ds(pl.multiple_of(frm * 8, 8), 8)], to, frm, band, to,
+        )
+
+    def row_bwd(t, _):
+        at = pl.ds(pl.multiple_of(t * span, span), span)
+        v = jnp.concatenate([xbuf[t * GROUP + i] for i in range(GROUP)], axis=0).astype(F32)
+        c = jnp.concatenate(
+            [
+                jnp.concatenate(
+                    [flat[lo, pl.ds(t * GROUP + i, L, stride=8), :] for lo in range(2)], axis=1
+                )
+                for i in range(GROUP)
+            ],
+            axis=0,
+        )
+        cb = c.astype(BF16)
+        do = dot_nt(cb, wro_ref[...]).astype(BF16)
+        qkv = qkvbuf[at]
+        backs = []
+        for i in range(GROUP):
+            own = qkv[i * L : (i + 1) * L]
+            backs.append(
+                attn_back(
+                    pbuf[t * GROUP + i], own[:, :D], own[:, D : 2 * D], own[:, 2 * D :],
+                    do[i * L : (i + 1) * L],
+                )
+            )
+        dqkv = jnp.concatenate(backs, axis=0)
+        dbuf[at] = dqkv
+        cbuf[at] = cb
+        dn = dot_nt(dqkv, wr_ref[...])
+        dv, ggain = norm_back(v, c, dn, gain_r)
+        gacc[0:1, :] += ggain
+        dvb = dv.astype(BF16)
+        which = ctin[0, pl.ds((t * GROUP) // 4, 1), :]
+        rows_of = lax.broadcasted_iota(jnp.int32, (CT, L), 0).astype(F32)
+        hot = jnp.where(rows_of == which, 1.0, 0.0).astype(BF16)
+        for i in range(GROUP):
+            gisend[t * GROUP + i] = dvb[i * L : (i + 1) * L]
+            ctacc[...] += dot_nn(hot, dvb[i * L : (i + 1) * L])
+        return 0
+
+    lax.fori_loop(0, 8 // GROUP, row_bwd, 0)
+
+    weight_grads(0, 0)
+    every(lambda i: rs_send(0, i).start(), ND)
+    every(lambda i: gi_copy(ring(i), block).start(), NB)
+    gi_ref[pl.ds(pl.multiple_of(block * 8, 8), 8)] = gisend[:, pl.ds(pl.multiple_of(block * 16, 16), 16)]
+
+    def cx_send(i):
+        o_, b, k = peer(i)
+        return remote(10, rows8(ctacc, o_), ctrecv.at[me], o_, me, b, k)
+
+    def cx_recv(i):
+        o_, b, k = peer(i)
+        return remote(10, rows8(ctacc, me), ctrecv.at[o_], o_, o_, b, k)
+
+    def gg_send(i):
+        o_, b, k = peer(i)
+        return remote(11, gacc, grecv.at[me], o_, me, b, k)
+
+    def gg_recv(i):
+        o_, b, k = peer(i)
+        return remote(11, gacc, grecv.at[o_], o_, o_, b, k)
+
+    every(lambda i: cx_send(i).start(), ND)
+    every(lambda i: gg_send(i).start(), ND)
+    reduce_own(1)
+    reduce_own(0)
+    ctrecv[me] = ctacc[pl.ds(pl.multiple_of(me * 8, 8), 8)]
+    grecv[me] = gacc[...]
+    every(lambda i: cx_recv(i).wait_recv(), ND)
+    every(lambda i: gg_recv(i).wait_recv(), ND)
+    total, gtotal = ctrecv[0], grecv[0]
+    for j in range(1, ND):
+        total = total + ctrecv[j]
+        gtotal = gtotal + grecv[j]
+    ctx_ref[...] = 0.25 * total
+    gg_ref[...] = gtotal * scaling
+    every(lambda i: ag_recv(1, i).wait_recv(), ND)
+    gc_ref[...] = wfull[1].astype(F32)
+    every(lambda i: ag_recv(0, i).wait_recv(), ND)
+    gr_ref[...] = wfull[0].astype(F32)
+    every(lambda i: gi_copy(block, ring(i)).wait_recv(), NB)
+
+    every(lambda i: in_copy(ring(i), block).wait_send(), NB)
+    every(lambda i: ct_copy(ring(i), block).wait_send(), NB)
+    g_copy(other, band).wait_send()
+    every(lambda i: h_send(i).wait_send(), ND)
+    every(lambda i: gh_send(i).wait_send(), ND)
+    for slot in range(2):
+        every(lambda i: rs_send(slot, i).wait_send(), ND)
+        every(lambda i: ag_send(slot, i).wait_send(), ND)
+    every(lambda i: gi_copy(ring(i), block).wait_send(), NB)
+    every(lambda i: cx_send(i).wait_send(), ND)
+    every(lambda i: gg_send(i).wait_send(), ND)
+
+
+def fused_shards(grid_input, grad_output, context_tile, gains, row_weights, column_weights):
+    cell_count = grid_input.shape[0] * grid_input.shape[1] * ND
+    scaling = 1.0 / math.sqrt(cell_count)
+    block = lax.axis_index("block")
+    cells = jnp.repeat(context_tile.astype(F32), 4, axis=1).reshape(NB, 2, 16)
+    lanes = jnp.tile(cells, (1, 1, NB))
+    mine = (lax.iota(jnp.int32, L) // 16) == block
+    placed = jnp.pad(jnp.where(mine, lanes, 0.0), ((0, 0), (0, 6), (0, 0)))
+    wr = jnp.concatenate([row_weights[0], row_weights[1], row_weights[2]], axis=1)
+    wc = jnp.concatenate([column_weights[0], column_weights[1], column_weights[2]], axis=1)
+    vm = pl.BlockSpec(memory_space=pltpu.VMEM)
+    big = lambda n, d=D, t=BF16: pltpu.VMEM((n, d), t)
+    outs = pl.pallas_call(
+        functools.partial(fused_kernel, scaling),
+        out_shape=(
+            jax.ShapeDtypeStruct((64, 16, D), BF16),
+            jax.ShapeDtypeStruct((1024, D), F32),
+            jax.ShapeDtypeStruct((1024, D), F32),
+            jax.ShapeDtypeStruct((8, D), F32),
+            jax.ShapeDtypeStruct((TILE_DEV, D), F32),
+        ),
+        in_specs=[vm] * 8,
+        out_specs=(vm,) * 5,
+        scratch_shapes=[
+            pltpu.VMEM((8, L, D), BF16),
+            pltpu.VMEM((NB, 8, L), F32),
+            pltpu.VMEM((2, 1024, L), F32),
+            big(1024), big(1024), big(1024), big(1024),
+            pltpu.VMEM((ND, 8, 8, D), F32),
+            pltpu.VMEM((ND, 8, 8, D), F32),
+            big(1024), big(1024),
+            big(2048), big(2048), big(1024, 3 * D),
+            pltpu.VMEM((8, HEADS * L, L), BF16),
+            big(2048, 3 * D), big(2048),
+            pltpu.VMEM((8, L, D), BF16),
+            pltpu.VMEM((2, 1024, D), BF16),
+            pltpu.VMEM((2, ND, 64, D), BF16),
+            pltpu.VMEM((2, 1024, D), BF16),
+            big(CT, D, F32),
+            pltpu.VMEM((ND, TILE_DEV, D), F32),
+            big(8, D, F32),
+            pltpu.VMEM((ND, 8, D), F32),
+            pltpu.SemaphoreType.DMA((12, ND)),
+            pltpu.SemaphoreType.DMA((12, ND)),
+        ],
+        compiler_params=pltpu.CompilerParams(
+            collective_id=0, has_side_effects=True, vmem_limit_bytes=56 * 1024 * 1024
+        ),
+    )(grid_input, grad_output, placed, gains, wr, row_weights[3], wc, column_weights[3])
+    grad_input, grad_row, grad_col, grad_gain, grad_context = outs
+    return (
+        grad_input,
+        grad_row.reshape(4, D, D),
+        grad_col.reshape(4, D, D),
+        grad_gain[:2],
+        grad_context,
+    )
+
+
 def solution(mesh):
     in_specs = (
         P(("parts", "band"), "block", None),
@@ -220,4 +697,5 @@
         P("parts", None),
         P(("parts", "band", "block"), None),
     )
-    return jax.shard_map(shards, mesh=mesh, in_specs=in_specs, out_specs=out_specs, check_vma=False)
+    chosen = fused_shards if fits_fused(mesh) else shards
+    return jax.shard_map(chosen, mesh=mesh, in_specs=in_specs, out_specs=out_specs, check_vma=False)

time: 486 us -> 142 us (0.29); the launches traced: 479 us -> 142 us
  matrix products: 206 us -> 0 us
  Pallas kernels: 0 us -> 130 us
  waiting for transfers between devices: 121 us -> 0 us
  local copies, waits for them, and re-layouts: 58.4 us -> 10.6 us
  blocking collectives: 41.4 us -> 0 us
  starting transfers between devices: 23.2 us -> 0 us
  between operations: 14.6 us -> 0.7 us
  other arithmetic: 13.1 us -> 0.94 us
    dot_general x108 -> x0, matrix products: 166 us -> none  [the longest x24 42.4 us: head_attend(): jnp.einsum('lbd,mbd->blm', queries, key_rows, preferred_element_type=jnp....]
    pallas_call x0 -> x1, Pallas kernels: none -> 130 us  [fused_shards(): pl.pallas_call(functools.partial(fused_kernel, scaling), out_shape=(jax.S...]
    psum x1 -> x0, waiting for transfers between devices: 66.6 us -> none  [shards(): lax.psum((row_terms, col_terms, gain_terms), ('band', 'block'))]
    all_to_all x5 -> x0, waiting for transfers between devices: 54.6 us -> none  [the longest x1 36 us: shards(): lax.all_to_all(packed_one, 'block', split_axis=0, concat_axis=1, tiled=True)]
    sub x32 -> x0, matrix products: 39.7 us -> none  [head_attend(): jax.nn.softmax(scores * scaling, axis=-1).astype(jnp.bfloat16)]
    psum x1 -> x0, blocking collectives: 33 us -> none  [shards(): lax.psum((row_terms, col_terms, gain_terms), ('band', 'block'))]
    all_to_all x5 -> x0, starting transfers between devices: 23.2 us -> none  [the longest x1 7.41 us: shards(): lax.all_to_all(packed_one, 'block', split_axis=0, concat_axis=1, tiled=True)]
    while x8 -> x0, local copies, waits for them, and re-layouts: 9.24 us -> none  [the longest x5 7.51 us: attend_back(): lax.map(single_head, (queries, key_rows, values, cotangents))]
  transfers between devices with their start and end apart: 6 -> 0, of which waited for: 4 -> 0; matrix products, arithmetic and copies ran while one was open for 16% -> 0% of each run, Pallas kernels for 0% -> 0%
where the time goes in v1:
time: 142 us
  Pallas kernels  130 us (92%)
  local copies, waits for them, and re-layouts  10.6 us (7%)
    pallas_call x1, Pallas kernels, fused_shards(): pl.pallas_call(functools.partial(fused_kernel, scaling), out_shape=(jax.S...  130 us
    unnamed x14, local copies, waits for them, and re-layouts  5.71 us

profile of v1, /device:TPU:0, one launch (start us, length us, event | category | flops | bytes accessed | tf_op | source)
XLA Modules:
  0.0 142.1 jit_solution(991804934840481886)
XLA Ops:
  0.6 0.0 copy-start.4
  0.7 0.7 copy-done.4
  1.3 0.1 copy.12
  1.4 0.1 broadcast_in_dim.12
  1.5 0.1 tile.10
  1.6 0.1 tile.12
  1.7 0.6 pad.4.ct_ref
  2.3 0.0 copy-start.2
  2.3 1.8 %slice_bitcast_fusion.4 = (bf16[256,256]{1,0:T(8,128)(2,1)}, bf16[256,256]{1,0:T(8,128)(2,1)S(1)}, bf16[256,256]{1,0:T(8,128)(2,1)S(1)}, bf16[256,256]{1,0:T(8,128)(2,1)S(1)}) fusion(bf16[4,256,256]{2,1,0:T(8,128)(2,1)} %param.10), kind=kLoop, calls=%fused_computation.6 | loop fusion | bytes 1048576 | tf_op jit(solution)/shard_map/squeeze | solution.py:673
  4.2 0.0 copy-done.2
  4.2 0.7 slice_bitcast_fusion
  4.9 0.9 pad_maximum_fusion
  5.8 129.9 %shard_map.101 = (bf16[64,16,256]{2,1,0:T(8,128)(2,1)}, f32[1024,256]{1,0:T(8,128)}, f32[1024,256]{1,0:T(8,128)}, f32[8,256]{1,0:T(8,128)}, f32[8,256]{1,0:T(8,128)}) custom-call(bf16[64,16,256]{2,1,0:T(8,128)(2,1)} %x_ref.1, bf16[64,16,256]{2,1,0:T(8,128)(2,1)} %g_ref.1, f32[8,8,128]{2,1,0:T(8,128)} %pad.4.ct_ref, f32[2,256]{1,0:T(2,128)} %gains_ref.1, ...), custom_call_target="tpu_custom_call" | custom-call | tf_op jit(solution)/shard_map/pallas_call | solution.py:637
  135.7 0.0 copy-start.1
  135.7 1.4 slice.35
  137.1 1.9 %copy.17 = bf16[64,16,256]{2,1,0:T(8,128)(2,1)} copy(bf16[64,16,256]{2,1,0:T(8,128)(2,1)} %get-tuple-element.30) | data formatting | bytes 1048576
  138.9 0.0 copy-done.1
  138.9 0.0 copy-start
  138.9 1.0 copy.18
  139.9 0.6 copy-done
  140.5 0.0 copy-start.3
  140.5 1.0 copy.19
  141.5 0.0 copy-done.3
  141.5 0.6 copy.20
  (4 shorter events, 0.0 us)
Async XLA Ops:
  0.6 0.7 copy-start.4
  2.3 1.8 %copy-start.2 = (bf16[4,256,256]{2,1,0:T(8,128)(2,1)S(1)}, bf16[4,256,256]{2,1,0:T(8,128)(2,1)}, u32[]{:S(2)}) copy-start(bf16[4,256,256]{2,1,0:T(8,128)(2,1)} %param.11) | copy-start | bytes 1572868
  135.7 3.2 %copy-start.1 = (f32[1024,256]{1,0:T(8,128)S(1)}, f32[1024,256]{1,0:T(8,128)}, u32[]{:S(2)}) copy-start(f32[1024,256]{1,0:T(8,128)} %get-tuple-element.11) | copy-start | bytes 3145732
  138.9 1.6 %copy-start = (f32[1024,256]{1,0:T(8,128)S(1)}, f32[1024,256]{1,0:T(8,128)}, u32[]{:S(2)}) copy-start(f32[1024,256]{1,0:T(8,128)} %get-tuple-element.12) | copy-start | bytes 3145732
  140.5 1.0 copy-start.3

commit v2 on v1

--- a/solution.py
+++ b/solution.py
@@ -291,11 +291,11 @@
 
 def fused_kernel(
     scaling,
-    x_ref, g_ref, ct_ref, gains_ref, wr_ref, wro_ref, wc_ref, wco_ref,
+    x_ref, g_ref, ct_ref, gains_ref, rw_ref, cw_ref,
     gi_ref, gr_ref, gc_ref, gg_ref, ctx_ref,
     xbuf, ctin, flat, gsend, gcol, hsend, hrecv, cols, cots, ghsend, ghrecv,
     nbuf, obuf, qkvbuf, pbuf, dbuf, cbuf, gisend,
-    wsend, wrecv, wfull, ctacc, ctrecv, gacc, grecv,
+    wsend, wpair, wred, wrecv, wfull, ctacc, ctpair, ctrecv, gacc, gpair, grecv, wr_ref, wc_ref,
     send_sem, recv_sem,
 ):
     band, block = lax.axis_index("band"), lax.axis_index("block")
@@ -337,19 +337,26 @@
     every(greet, ND)
     pl.semaphore_wait(barrier, ND - 1)
 
-    def in_copy(to, frm):
+    def in_copy(t, to, frm):
         return remote(
-            0, x_ref.at[pl.ds(pl.multiple_of(to * 8, 8), 8)],
-            xbuf.at[:, pl.ds(pl.multiple_of(frm * 16, 16), 16)], to, frm, band, to,
+            t, x_ref.at[pl.ds(to * 8 + t * GROUP, GROUP)],
+            xbuf.at[pl.ds(t * GROUP, GROUP), pl.ds(pl.multiple_of(frm * 16, 16), 16)],
+            to, frm, band, to,
         )
 
     def ct_copy(to, frm):
-        return remote(1, ct_ref.at[to], ctin.at[frm], to, frm, band, to)
+        return remote(4, ct_ref.at[to], ctin.at[frm], to, frm, band, to)
 
     def ring(i):
         return lax.rem(block + i, NB)
 
-    every(lambda i: in_copy(ring(i), block).start(), NB)
+    def groups(fn, least=0, most=8 // GROUP):
+        def step(t, _):
+            fn(t)
+            return 0
+        lax.fori_loop(least, most, step, 0)
+
+    groups(lambda t: every(lambda i: in_copy(t, ring(i), block).start(), NB))
     every(lambda i: ct_copy(ring(i), block).start(), NB)
     xbuf[:, pl.ds(pl.multiple_of(block * 16, 16), 16)] = x_ref[pl.ds(pl.multiple_of(block * 8, 8), 8)]
     ctin[block] = ct_ref[block]
@@ -372,19 +379,22 @@
         return ref.at[pl.ds(pl.multiple_of(j * 512, 512), 512)]
 
     def g_copy(to, frm):
-        return remote(2, half512(gsend, to), half512(gcol, frm), to, frm, to, block)
+        return remote(5, half512(gsend, to), half512(gcol, frm), to, frm, to, block)
 
     other = 1 - band
     g_copy(other, band).start()
     gcol[pl.ds(pl.multiple_of(band * 512, 512), 512)] = gsend[pl.ds(pl.multiple_of(band * 512, 512), 512)]
 
-    every(lambda i: in_copy(block, ring(i)).wait_recv(), NB)
+    for m in range(3):
+        wr_ref[:, m * D : (m + 1) * D] = rw_ref[m]
+        wc_ref[:, m * D : (m + 1) * D] = cw_ref[m]
 
     gain_r = gains_ref[0:1, :]
     gain_c = gains_ref[1:2, :]
     span = GROUP * L
 
     def row_fwd(t, _):
+        every(lambda i: in_copy(t, block, ring(i)).wait_recv(), NB)
         at = pl.ds(pl.multiple_of(t * span, span), span)
         v = jnp.concatenate([xbuf[t * GROUP + i] for i in range(GROUP)], axis=0).astype(F32)
         u, _inv = norm_parts(v)
@@ -400,7 +410,7 @@
         nbuf[at] = n
         obuf[at] = o
         qkvbuf[at] = qkv
-        hidden = v + dot_nn(o, wro_ref[...])
+        hidden = v + dot_nn(o, rw_ref[3])
         for i in range(GROUP):
             for lo in range(2):
                 flat[lo, pl.ds(t * GROUP + i, L, stride=8), :] = hidden[
@@ -412,20 +422,21 @@
     for lo in range(2):
         hsend[:, lo * L : lo * L + L] = flat[lo].astype(BF16)
 
-    def h_send(i):
+    def part32(ref, j, u):
+        return ref.at[pl.ds(pl.multiple_of(j * 64 + u * 32, 32), 32)]
+
+    def h_send(u, i):
         o_, b, k = peer(i)
-        return remote(3, rows64(hsend, 2 * k + b), rows64(hrecv, me), o_, me, b, k)
-
-    def h_recv(i):
+        return remote(6 + u, part32(hsend, 2 * k + b, u), part32(hrecv, me, u), o_, me, b, k)
+
+    def h_recv(u, i):
         o_, b, k = peer(i)
-        return remote(3, rows64(hsend, mycol), rows64(hrecv, o_), o_, o_, b, k)
-
-    every(lambda i: h_send(i).start(), ND)
+        return remote(6 + u, part32(hsend, mycol, u), part32(hrecv, o_, u), o_, o_, b, k)
+
+    groups(lambda u: every(lambda i: h_send(u, i).start(), ND), 0, 2)
     hrecv[pl.ds(pl.multiple_of(me * 64, 64), 64)] = hsend[pl.ds(pl.multiple_of(mycol * 64, 64), 64)]
     g_copy(band, other).wait_recv()
     cots[...] = gcol[...].astype(F32).reshape(ND, 8, 8, D)
-    every(lambda i: h_recv(i).wait_recv(), ND)
-    cols[...] = hrecv[...].astype(F32).reshape(ND, 8, 8, D)
 
     gacc[...] = jnp.zeros_like(gacc)
 
@@ -437,7 +448,7 @@
         u, _inv = norm_parts(v)
         n = (u * gain_c).astype(BF16)
         qkv = dot_nn(n, wc_ref[...]).astype(BF16)
-        do = dot_nt(cb, wco_ref[...]).astype(BF16)
+        do = dot_nt(cb, cw_ref[3]).astype(BF16)
         outs, backs = [], []
         for i in range(GROUP):
             own = qkv[i * L : (i + 1) * L]
@@ -452,23 +463,40 @@
         cbuf[at] = cb
         dn = dot_nt(dqkv, wc_ref[...])
         dv, ggain = norm_back(v, c, dn, gain_c)
-        gacc[1:2, :] += ggain
+        gacc[2:3, :] += ggain[:, :L]
+        gacc[3:4, :] += ggain[:, L:]
         for i in range(GROUP):
             cols[:, t * GROUP + i] = dv[i * L : (i + 1) * L].reshape(ND, 8, D)
         return 0
 
-    lax.fori_loop(0, 8 // GROUP, col_step, 0)
-    ghsend[...] = cols[...].reshape(1024, D).astype(BF16)
-
-    def gh_send(i):
+    def gh_send(u, i):
         o_, b, k = peer(i)
-        return remote(4, rows64(ghsend, o_), rows64(ghrecv, mycol), o_, me, b, k)
-
-    def gh_recv(i):
+        return remote(8 + u, part32(ghsend, o_, u), part32(ghrecv, mycol, u), o_, me, b, k)
+
+    def gh_recv(u, i):
         o_, b, k = peer(i)
-        return remote(4, rows64(ghsend, me), rows64(ghrecv, 2 * k + b), o_, o_, b, k)
-
-    every(lambda i: gh_send(i).start(), ND)
+        return remote(8 + u, part32(ghsend, me, u), part32(ghrecv, 2 * k + b, u), o_, o_, b, k)
+
+    def col_half(u):
+        every(lambda i: h_recv(u, i).wait_recv(), ND)
+
+        def take(j, _):
+            at = pl.ds(pl.multiple_of(j * 64 + u * 32, 32), 32)
+            cols[j, pl.ds(u * 4, 4)] = hrecv[at].astype(F32).reshape(4, 8, D)
+            return 0
+
+        lax.fori_loop(0, ND, take, 0)
+        lax.fori_loop(u * (4 // GROUP), (u + 1) * (4 // GROUP), col_step, 0)
+
+        def give(j, _):
+            at = pl.ds(pl.multiple_of(j * 64 + u * 32, 32), 32)
+            ghsend[at] = cols[j, pl.ds(u * 4, 4)].reshape(32, D).astype(BF16)
+            return 0
+
+        lax.fori_loop(0, ND, give, 0)
+        every(lambda i: gh_send(u, i).start(), ND)
+
+    groups(col_half, 0, 2)
     ghrecv[pl.ds(pl.multiple_of(mycol * 64, 64), 64)] = ghsend[pl.ds(pl.multiple_of(me * 64, 64), 64)]
 
     def weight_grads(start, slot):
@@ -480,33 +508,42 @@
             ).astype(BF16)
         wsend[slot, 3 * D : 4 * D] = (dot_tn(obuf[span_all], cbuf[span_all]) * scaling).astype(BF16)
 
-    def rs_send(slot, i):
-        o_, b, k = peer(i)
-        return remote(5 + slot, rows64(wsend.at[slot], o_), wrecv.at[slot, me], o_, me, b, k)
-
-    def rs_recv(slot, i):
-        o_, b, k = peer(i)
-        return remote(5 + slot, rows64(wsend.at[slot], me), wrecv.at[slot, o_], o_, o_, b, k)
-
-    def ag_send(slot, i):
-        o_, b, k = peer(i)
-        return remote(7 + slot, rows64(wfull.at[slot], me), rows64(wfull.at[slot], me), o_, me, b, k)
-
-    def ag_recv(slot, i):
-        o_, b, k = peer(i)
-        return remote(7 + slot, rows64(wfull.at[slot], me), rows64(wfull.at[slot], o_), o_, o_, b, k)
+    def pair_copy(slot, to, frm):
+        return remote(14 + slot, half512(wsend.at[slot], to), wpair.at[slot], to, frm, to, block)
+
+    def back_copy(slot, to, frm):
+        return remote(
+            16 + slot, half512(wfull.at[slot], frm), half512(wfull.at[slot], frm), to, frm, to, block
+        )
+
+    def rs_copy(slot, to, frm):
+        return remote(10 + slot, rows64(wred.at[slot], to), wrecv.at[slot, frm], to, frm, band, to)
+
+    def ag_copy(slot, to, frm):
+        own = rows64(wfull.at[slot], band * NB + frm)
+        return remote(12 + slot, own, own, to, frm, band, to)
+
+    def reduce_pair(slot):
+        pair_copy(slot, band, other).wait_recv()
+        own = wsend[slot, pl.ds(pl.multiple_of(band * 512, 512), 512)].astype(F32)
+        wred[slot] = (own + wpair[slot].astype(F32)).astype(BF16)
+        every(lambda i: rs_copy(slot, ring(i), block).start(), NB)
 
     def reduce_own(slot):
-        every(lambda i: rs_recv(slot, i).wait_recv(), ND)
-        wrecv[slot, me] = wsend[slot, pl.ds(pl.multiple_of(me * 64, 64), 64)]
+        wrecv[slot, block] = wred[slot, pl.ds(pl.multiple_of(block * 64, 64), 64)]
+        every(lambda i: rs_copy(slot, block, ring(i)).wait_recv(), NB)
         total = wrecv[slot, 0].astype(F32)
-        for j in range(1, ND):
+        for j in range(1, NB):
             total = total + wrecv[slot, j].astype(F32)
         wfull[slot, pl.ds(pl.multiple_of(me * 64, 64), 64)] = total.astype(BF16)
-        every(lambda i: ag_send(slot, i).start(), ND)
+        every(lambda i: ag_copy(slot, ring(i), block).start(), NB)
+
+    def gather_back(slot):
+        every(lambda i: ag_copy(slot, block, ring(i)).wait_recv(), NB)
+        back_copy(slot, other, band).start()
 
     weight_grads(1024, 1)
-    every(lambda i: rs_send(1, i).start(), ND)
+    pair_copy(1, other, band).start()
 
     every(lambda i: ct_copy(block, ring(i)).wait_recv(), NB)
     tiles = ctin[0]
@@ -515,16 +552,18 @@
     tile_ids = tiles.astype(jnp.int32)
     ctin[0] = tile_ids.astype(F32)
 
-    every(lambda i: gh_recv(i).wait_recv(), ND)
+    groups(lambda u: every(lambda i: gh_recv(u, i).wait_recv(), ND), 0, 2)
+    reduce_pair(1)
     for lo in range(2):
         flat[lo] = ghrecv[:, lo * L : lo * L + L].astype(F32)
 
     ctacc[...] = jnp.zeros_like(ctacc)
 
-    def gi_copy(to, frm):
+    def gi_copy(t, to, frm):
         return remote(
-            9, gisend.at[:, pl.ds(pl.multiple_of(to * 16, 16), 16)],
-            gi_ref.at[pl.ds(pl.multiple_of(frm * 8, 8), 8)], to, frm, band, to,
+            18 + t,
+            gisend.at[pl.ds(t * GROUP, GROUP), pl.ds(pl.multiple_of(to * 16, 16), 16)],
+            gi_ref.at[pl.ds(frm * 8 + t * GROUP, GROUP)], to, frm, band, to,
         )
 
     def row_bwd(t, _):
@@ -540,7 +579,7 @@
             axis=0,
         )
         cb = c.astype(BF16)
-        do = dot_nt(cb, wro_ref[...]).astype(BF16)
+        do = dot_nt(cb, rw_ref[3]).astype(BF16)
         qkv = qkvbuf[at]
         backs = []
         for i in range(GROUP):
@@ -556,7 +595,8 @@
         cbuf[at] = cb
         dn = dot_nt(dqkv, wr_ref[...])
         dv, ggain = norm_back(v, c, dn, gain_r)
-        gacc[0:1, :] += ggain
+        gacc[0:1, :] += ggain[:, :L]
+        gacc[1:2, :] += ggain[:, L:]
         dvb = dv.astype(BF16)
         which = ctin[0, pl.ds((t * GROUP) // 4, 1), :]
         rows_of = lax.broadcasted_iota(jnp.int32, (CT, L), 0).astype(F32)
@@ -564,62 +604,77 @@
         for i in range(GROUP):
             gisend[t * GROUP + i] = dvb[i * L : (i + 1) * L]
             ctacc[...] += dot_nn(hot, dvb[i * L : (i + 1) * L])
+        every(lambda i: gi_copy(t, ring(i), block).start(), NB)
         return 0
 
     lax.fori_loop(0, 8 // GROUP, row_bwd, 0)
 
     weight_grads(0, 0)
-    every(lambda i: rs_send(0, i).start(), ND)
-    every(lambda i: gi_copy(ring(i), block).start(), NB)
+    pair_copy(0, other, band).start()
+
+    def half64(ref, j):
+        return ref.at[pl.ds(pl.multiple_of(j * 64, 64), 64)]
+
+    def cx_pair(to, frm):
+        return remote(24, half64(ctacc, to), ctpair, to, frm, to, block)
+
+    def cx_copy(to, frm):
+        return remote(22, rows8(ctacc, band * NB + to), ctrecv.at[frm], to, frm, band, to)
+
+    def gg_pair(to, frm):
+        return remote(25, gacc, gpair, to, frm, to, block)
+
+    def gg_copy(to, frm):
+        return remote(23, gpair, grecv.at[frm], to, frm, band, to)
+
+    cx_pair(other, band).start()
+    gg_pair(other, band).start()
+    reduce_pair(0)
+    reduce_own(1)
     gi_ref[pl.ds(pl.multiple_of(block * 8, 8), 8)] = gisend[:, pl.ds(pl.multiple_of(block * 16, 16), 16)]
-
-    def cx_send(i):
-        o_, b, k = peer(i)
-        return remote(10, rows8(ctacc, o_), ctrecv.at[me], o_, me, b, k)
-
-    def cx_recv(i):
-        o_, b, k = peer(i)
-        return remote(10, rows8(ctacc, me), ctrecv.at[o_], o_, o_, b, k)
-
-    def gg_send(i):
-        o_, b, k = peer(i)
-        return remote(11, gacc, grecv.at[me], o_, me, b, k)
-
-    def gg_recv(i):
-        o_, b, k = peer(i)
-        return remote(11, gacc, grecv.at[o_], o_, o_, b, k)
-
-    every(lambda i: cx_send(i).start(), ND)
-    every(lambda i: gg_send(i).start(), ND)
-    reduce_own(1)
+    cx_pair(band, other).wait_recv()
+    mine64 = pl.ds(pl.multiple_of(band * 64, 64), 64)
+    ctacc[mine64] = ctacc[mine64] + ctpair[...]
+    gg_pair(band, other).wait_recv()
+    gpair[...] = gpair[...] + gacc[...]
+    every(lambda i: cx_copy(ring(i), block).start(), NB)
+    every(lambda i: gg_copy(ring(i), block).start(), NB)
+    ctrecv[block] = ctacc[pl.ds(pl.multiple_of(me * 8, 8), 8)]
+    grecv[block] = gpair[...]
     reduce_own(0)
-    ctrecv[me] = ctacc[pl.ds(pl.multiple_of(me * 8, 8), 8)]
-    grecv[me] = gacc[...]
-    every(lambda i: cx_recv(i).wait_recv(), ND)
-    every(lambda i: gg_recv(i).wait_recv(), ND)
+    gather_back(1)
+    every(lambda i: cx_copy(block, ring(i)).wait_recv(), NB)
+    every(lambda i: gg_copy(block, ring(i)).wait_recv(), NB)
     total, gtotal = ctrecv[0], grecv[0]
-    for j in range(1, ND):
+    for j in range(1, NB):
         total = total + ctrecv[j]
         gtotal = gtotal + grecv[j]
     ctx_ref[...] = 0.25 * total
-    gg_ref[...] = gtotal * scaling
-    every(lambda i: ag_recv(1, i).wait_recv(), ND)
-    gc_ref[...] = wfull[1].astype(F32)
-    every(lambda i: ag_recv(0, i).wait_recv(), ND)
-    gr_ref[...] = wfull[0].astype(F32)
-    every(lambda i: gi_copy(block, ring(i)).wait_recv(), NB)
-
-    every(lambda i: in_copy(ring(i), block).wait_send(), NB)
+    gtotal = gtotal * scaling
+    for m in range(2):
+        gg_ref[m : m + 1, :] = jnp.concatenate([gtotal[2 * m : 2 * m + 1], gtotal[2 * m + 1 : 2 * m + 2]], axis=1)
+    back_copy(1, band, other).wait_recv()
+    gc_ref[...] = wfull[1].astype(F32).reshape(4, D, D)
+    gather_back(0)
+    groups(lambda t: every(lambda i: gi_copy(t, block, ring(i)).wait_recv(), NB))
+    back_copy(0, band, other).wait_recv()
+    gr_ref[...] = wfull[0].astype(F32).reshape(4, D, D)
+
+    groups(lambda t: every(lambda i: in_copy(t, ring(i), block).wait_send(), NB))
     every(lambda i: ct_copy(ring(i), block).wait_send(), NB)
     g_copy(other, band).wait_send()
-    every(lambda i: h_send(i).wait_send(), ND)
-    every(lambda i: gh_send(i).wait_send(), ND)
+    groups(lambda u: every(lambda i: h_send(u, i).wait_send(), ND), 0, 2)
+    groups(lambda u: every(lambda i: gh_send(u, i).wait_send(), ND), 0, 2)
     for slot in range(2):
-        every(lambda i: rs_send(slot, i).wait_send(), ND)
-        every(lambda i: ag_send(slot, i).wait_send(), ND)
-    every(lambda i: gi_copy(ring(i), block).wait_send(), NB)
-    every(lambda i: cx_send(i).wait_send(), ND)
-    every(lambda i: gg_send(i).wait_send(), ND)
+        pair_copy(slot, other, band).wait_send()
+        back_copy(slot, other, band).wait_send()
+        every(lambda i: rs_copy(slot, ring(i), block).wait_send(), NB)
+        every(lambda i: ag_copy(slot, ring(i), block).wait_send(), NB)
+    groups(lambda t: every(lambda i: gi_copy(t, ring(i), block).wait_send(), NB))
+    cx_pair(other, band).wait_send()
+    gg_pair(other, band).wait_send()
+    every(lambda i: cx_copy(ring(i), block).wait_send(), NB)
+    every(lambda i: gg_copy(ring(i), block).wait_send(), NB)
 
 
 def fused_shards(grid_input, grad_output, context_tile, gains, row_weights, column_weights):
@@ -630,20 +685,18 @@
     lanes = jnp.tile(cells, (1, 1, NB))
     mine = (lax.iota(jnp.int32, L) // 16) == block
     placed = jnp.pad(jnp.where(mine, lanes, 0.0), ((0, 0), (0, 6), (0, 0)))
-    wr = jnp.concatenate([row_weights[0], row_weights[1], row_weights[2]], axis=1)
-    wc = jnp.concatenate([column_weights[0], column_weights[1], column_weights[2]], axis=1)
     vm = pl.BlockSpec(memory_space=pltpu.VMEM)
     big = lambda n, d=D, t=BF16: pltpu.VMEM((n, d), t)
     outs = pl.pallas_call(
         functools.partial(fused_kernel, scaling),
         out_shape=(
             jax.ShapeDtypeStruct((64, 16, D), BF16),
-            jax.ShapeDtypeStruct((1024, D), F32),
-            jax.ShapeDtypeStruct((1024, D), F32),
-            jax.ShapeDtypeStruct((8, D), F32),
+            jax.ShapeDtypeStruct((4, D, D), F32),
+            jax.ShapeDtypeStruct((4, D, D), F32),
+            jax.ShapeDtypeStruct((2, D), F32),
             jax.ShapeDtypeStruct((TILE_DEV, D), F32),
         ),
-        in_specs=[vm] * 8,
+        in_specs=[vm] * 6,
         out_specs=(vm,) * 5,
         scratch_shapes=[
             pltpu.VMEM((8, L, D), BF16),
@@ -658,27 +711,25 @@
             big(2048, 3 * D), big(2048),
             pltpu.VMEM((8, L, D), BF16),
             pltpu.VMEM((2, 1024, D), BF16),
-            pltpu.VMEM((2, ND, 64, D), BF16),
+            pltpu.VMEM((2, 512, D), BF16),
+            pltpu.VMEM((2, 512, D), BF16),
+            pltpu.VMEM((2, NB, 64, D), BF16),
             pltpu.VMEM((2, 1024, D), BF16),
             big(CT, D, F32),
-            pltpu.VMEM((ND, TILE_DEV, D), F32),
-            big(8, D, F32),
-            pltpu.VMEM((ND, 8, D), F32),
-            pltpu.SemaphoreType.DMA((12, ND)),
-            pltpu.SemaphoreType.DMA((12, ND)),
+            big(64, D, F32),
+            pltpu.VMEM((NB, TILE_DEV, D), F32),
+            big(8, L, F32),
+            big(8, L, F32),
+            pltpu.VMEM((NB, 8, L), F32),
+            big(D, 3 * D), big(D, 3 * D),
+            pltpu.SemaphoreType.DMA((26, ND)),
+            pltpu.SemaphoreType.DMA((26, ND)),
         ],
         compiler_params=pltpu.CompilerParams(
             collective_id=0, has_side_effects=True, vmem_limit_bytes=56 * 1024 * 1024
         ),
-    )(grid_input, grad_output, placed, gains, wr, row_weights[3], wc, column_weights[3])
-    grad_input, grad_row, grad_col, grad_gain, grad_context = outs
-    return (
-        grad_input,
-        grad_row.reshape(4, D, D),
-        grad_col.reshape(4, D, D),
-        grad_gain[:2],
-        grad_context,
-    )
+    )(grid_input, grad_output, placed, gains, row_weights, column_weights)
+    return outs
 
 
 def solution(mesh):

time: 142 us -> 108 us (0.76); the launches traced: 142 us -> 107 us
  Pallas kernels: 130 us -> 98.5 us
  local copies, waits for them, and re-layouts: 10.6 us -> 7.35 us
    pallas_call x1, Pallas kernels: 130 us -> 98.5 us  [fused_shards(): pl.pallas_call(functools.partial(fused_kernel, scaling), out_shape=(jax.S...]
    squeeze x2 -> x0, local copies, waits for them, and re-layouts: 2.52 us -> none  [the longest x1 1.84 us: fused_shards(): row_weights[3]]
    unnamed x14 -> x15, local copies, waits for them, and re-layouts: 5.71 us -> 6.38 us
where the time goes in v2:
time: 108 us; the launch traced here: 107 us
  Pallas kernels  98.5 us (91%)
  local copies, waits for them, and re-layouts  7.35 us (7%)
    pallas_call x1, Pallas kernels, fused_shards(): pl.pallas_call(functools.partial(fused_kernel, scaling), out_shape=(jax.S...  98.5 us
    unnamed x15, local copies, waits for them, and re-layouts  6.38 us

profile of v2, /device:TPU:0, one launch (start us, length us, event | category | flops | bytes accessed | tf_op | source)
XLA Modules:
  0.0 106.5 jit_solution(2273700805683070733)
XLA Ops:
  0.6 0.0 copy-start.3
  0.7 0.7 copy-done.3
  1.3 0.1 copy.12
  1.4 0.1 broadcast_in_dim.12
  1.5 0.1 tile.10
  1.6 0.1 tile.12
  1.7 0.6 pad.4.ct_ref
  2.3 98.5 %shard_map.101 = (bf16[64,16,256]{2,1,0:T(8,128)(2,1)}, f32[4,256,256]{2,1,0:T(8,128)}, f32[4,256,256]{2,1,0:T(8,128)}, f32[2,256]{1,0:T(2,128)}, f32[8,256]{1,0:T(8,128)}) custom-call(bf16[64,16,256]{2,1,0:T(8,128)(2,1)} %x_ref.1, bf16[64,16,256]{2,1,0:T(8,128)(2,1)} %g_ref.1, f32[8,8,128]{2,1,0:T(8,128)} %pad.4.ct_ref, f32[2,256]{1,0:T(2,128)} %gains_ref.1, ...), custom_call_target="tpu_custom_call" | custom-call | tf_op jit(solution)/shard_map/pallas_call | solution.py:690
  100.8 0.0 copy-start.1
  100.8 2.0 %copy.18 = bf16[64,16,256]{2,1,0:T(8,128)(2,1)} copy(bf16[64,16,256]{2,1,0:T(8,128)(2,1)} %get-tuple-element.10) | data formatting | bytes 1048576
  102.8 0.0 copy-done.1
  102.8 0.0 copy-start
  102.8 1.0 copy.19
  103.8 0.6 copy-done
  104.4 0.0 copy-start.4
  104.4 0.0 copy-start.2
  104.4 1.0 copy.20
  105.4 0.0 copy-done.4
  105.4 0.6 copy.21
  105.9 0.0 copy-done.2
  105.9 0.6 copy.22
  (4 shorter events, 0.0 us)
Async XLA Ops:
  0.6 0.7 copy-start.3
  100.8 2.0 %copy-start.1 = (f32[4,256,256]{2,1,0:T(8,128)S(1)}, f32[4,256,256]{2,1,0:T(8,128)}, u32[]{:S(2)}) copy-start(f32[4,256,256]{2,1,0:T(8,128)} %get-tuple-element.11) | copy-start | bytes 3145732
  102.8 1.6 %copy-start = (f32[4,256,256]{2,1,0:T(8,128)S(1)}, f32[4,256,256]{2,1,0:T(8,128)}, u32[]{:S(2)}) copy-start(f32[4,256,256]{2,1,0:T(8,128)} %get-tuple-element.12) | copy-start | bytes 3145732
  104.4 1.0 copy-start.4
  104.4 1.6 %copy-start.2 = (f32[8,256]{1,0:T(8,128)S(1)}, f32[8,256]{1,0:T(8,128)}, u32[]{:S(2)}) copy-start(f32[8,256]{1,0:T(8,128)} %get-tuple-element.14) | copy-start | bytes 24580

commit v3 on v2

--- a/solution.py
+++ b/solution.py
@@ -295,7 +295,7 @@
     gi_ref, gr_ref, gc_ref, gg_ref, ctx_ref,
     xbuf, ctin, flat, gsend, gcol, hsend, hrecv, cols, cots, ghsend, ghrecv,
     nbuf, obuf, qkvbuf, pbuf, dbuf, cbuf, gisend,
-    wsend, wpair, wred, wrecv, wfull, ctacc, ctpair, ctrecv, gacc, gpair, grecv, wr_ref, wc_ref,
+    wsend, wpair, wred, wside, wquart, wrecv, wfull, ctacc, ctpair, ctrecv, gacc, gpair, grecv, wr_ref, wc_ref,
     send_sem, recv_sem,
 ):
     band, block = lax.axis_index("band"), lax.axis_index("block")
@@ -516,30 +516,64 @@
             16 + slot, half512(wfull.at[slot], frm), half512(wfull.at[slot], frm), to, frm, to, block
         )
 
+    near, far = lax.rem(block, 2), block // 2
+    across = 2 * far + 1 - near
+    quarter = pl.multiple_of(band * 512 + near * 256, 256)
+    across_quarter = pl.multiple_of(band * 512 + (1 - near) * 256, 256)
+    own_at = pl.multiple_of(band * 512 + near * 256 + far * 64, 64)
+    NF = NB // 2
+
+    def far_ring(i):
+        return lax.rem(far + i, NF)
+
+    def side_copy(slot, to, frm):
+        return remote(
+            26 + slot, wred.at[slot, pl.ds(pl.multiple_of((1 - near) * 256, 256), 256)],
+            wside.at[slot], to, frm, band, to,
+        )
+
+    def side_back(slot, to, frm, at):
+        part = wfull.at[slot, pl.ds(at, 256)]
+        return remote(28 + slot, part, part, to, frm, band, to)
+
     def rs_copy(slot, to, frm):
-        return remote(10 + slot, rows64(wred.at[slot], to), wrecv.at[slot, frm], to, frm, band, to)
+        return remote(
+            10 + slot, rows64(wquart.at[slot], to), wrecv.at[slot, frm], to, frm,
+            band, 2 * to + near,
+        )
 
     def ag_copy(slot, to, frm):
-        own = rows64(wfull.at[slot], band * NB + frm)
-        return remote(12 + slot, own, own, to, frm, band, to)
+        at = pl.multiple_of(band * 512 + near * 256 + frm * 64, 64)
+        own = wfull.at[slot, pl.ds(at, 64)]
+        return remote(12 + slot, own, own, to, frm, band, 2 * to + near)
 
     def reduce_pair(slot):
         pair_copy(slot, band, other).wait_recv()
         own = wsend[slot, pl.ds(pl.multiple_of(band * 512, 512), 512)].astype(F32)
         wred[slot] = (own + wpair[slot].astype(F32)).astype(BF16)
-        every(lambda i: rs_copy(slot, ring(i), block).start(), NB)
+        side_copy(slot, across, block).start()
+
+    def reduce_side(slot):
+        side_copy(slot, block, across).wait_recv()
+        own = wred[slot, pl.ds(pl.multiple_of(near * 256, 256), 256)].astype(F32)
+        wquart[slot] = (own + wside[slot].astype(F32)).astype(BF16)
+        every(lambda i: rs_copy(slot, far_ring(i), far).start(), NF)
 
     def reduce_own(slot):
-        wrecv[slot, block] = wred[slot, pl.ds(pl.multiple_of(block * 64, 64), 64)]
-        every(lambda i: rs_copy(slot, block, ring(i)).wait_recv(), NB)
+        wrecv[slot, far] = wquart[slot, pl.ds(pl.multiple_of(far * 64, 64), 64)]
+        every(lambda i: rs_copy(slot, far, far_ring(i)).wait_recv(), NF)
         total = wrecv[slot, 0].astype(F32)
-        for j in range(1, NB):
+        for j in range(1, NF):
             total = total + wrecv[slot, j].astype(F32)
-        wfull[slot, pl.ds(pl.multiple_of(me * 64, 64), 64)] = total.astype(BF16)
-        every(lambda i: ag_copy(slot, ring(i), block).start(), NB)
+        wfull[slot, pl.ds(own_at, 64)] = total.astype(BF16)
+        every(lambda i: ag_copy(slot, far_ring(i), far).start(), NF)
+
+    def gather_side(slot):
+        every(lambda i: ag_copy(slot, far, far_ring(i)).wait_recv(), NF)
+        side_back(slot, across, block, quarter).start()
 
     def gather_back(slot):
-        every(lambda i: ag_copy(slot, block, ring(i)).wait_recv(), NB)
+        side_back(slot, block, across, across_quarter).wait_recv()
         back_copy(slot, other, band).start()
 
     weight_grads(1024, 1)
@@ -605,6 +639,11 @@
             gisend[t * GROUP + i] = dvb[i * L : (i + 1) * L]
             ctacc[...] += dot_nn(hot, dvb[i * L : (i + 1) * L])
         every(lambda i: gi_copy(t, ring(i), block).start(), NB)
+
+        @pl.when(t == 1)
+        def _():
+            reduce_side(1)
+
         return 0
 
     lax.fori_loop(0, 8 // GROUP, row_bwd, 0)
@@ -631,6 +670,7 @@
     gg_pair(other, band).start()
     reduce_pair(0)
     reduce_own(1)
+    reduce_side(0)
     gi_ref[pl.ds(pl.multiple_of(block * 8, 8), 8)] = gisend[:, pl.ds(pl.multiple_of(block * 16, 16), 16)]
     cx_pair(band, other).wait_recv()
     mine64 = pl.ds(pl.multiple_of(band * 64, 64), 64)
@@ -641,8 +681,10 @@
     every(lambda i: gg_copy(ring(i), block).start(), NB)
     ctrecv[block] = ctacc[pl.ds(pl.multiple_of(me * 8, 8), 8)]
     grecv[block] = gpair[...]
+    gather_side(1)
     reduce_own(0)
     gather_back(1)
+    gather_side(0)
     every(lambda i: cx_copy(block, ring(i)).wait_recv(), NB)
     every(lambda i: gg_copy(block, ring(i)).wait_recv(), NB)
     total, gtotal = ctrecv[0], grecv[0]
@@ -668,8 +710,10 @@
     for slot in range(2):
         pair_copy(slot, other, band).wait_send()
         back_copy(slot, other, band).wait_send()
-        every(lambda i: rs_copy(slot, ring(i), block).wait_send(), NB)
-        every(lambda i: ag_copy(slot, ring(i), block).wait_send(), NB)
+        side_copy(slot, across, block).wait_send()
+        side_back(slot, across, block, quarter).wait_send()
+        every(lambda i: rs_copy(slot, far_ring(i), far).wait_send(), NF)
+        every(lambda i: ag_copy(slot, far_ring(i), far).wait_send(), NF)
     groups(lambda t: every(lambda i: gi_copy(t, ring(i), block).wait_send(), NB))
     cx_pair(other, band).wait_send()
     gg_pair(other, band).wait_send()
@@ -713,7 +757,9 @@
             pltpu.VMEM((2, 1024, D), BF16),
             pltpu.VMEM((2, 512, D), BF16),
             pltpu.VMEM((2, 512, D), BF16),
-            pltpu.VMEM((2, NB, 64, D), BF16),
+            pltpu.VMEM((2, 256, D), BF16),
+            pltpu.VMEM((2, 256, D), BF16),
+            pltpu.VMEM((2, NB // 2, 64, D), BF16),
             pltpu.VMEM((2, 1024, D), BF16),
             big(CT, D, F32),
             big(64, D, F32),
@@ -722,8 +768,8 @@
             big(8, L, F32),
             pltpu.VMEM((NB, 8, L), F32),
             big(D, 3 * D), big(D, 3 * D),
-            pltpu.SemaphoreType.DMA((26, ND)),
-            pltpu.SemaphoreType.DMA((26, ND)),
+            pltpu.SemaphoreType.DMA((30, ND)),
+            pltpu.SemaphoreType.DMA((30, ND)),
         ],
         compiler_params=pltpu.CompilerParams(
             collective_id=0, has_side_effects=True, vmem_limit_bytes=56 * 1024 * 1024

time: 108 us -> 107 us (level)
  no operation moved by 1% of the time
where the time goes in v3:
time: 107 us; the launch traced here: 106 us
  Pallas kernels  97.7 us (91%)
  local copies, waits for them, and re-layouts  7.35 us (7%)
    pallas_call x1, Pallas kernels, fused_shards(): pl.pallas_call(functools.partial(fused_kernel, scaling), out_shape=(jax.S...  97.7 us
    unnamed x15, local copies, waits for them, and re-layouts  6.38 us

profile of v3, /device:TPU:0, one launch (start us, length us, event | category | flops | bytes accessed | tf_op | source)
XLA Modules:
  0.0 105.8 jit_solution(10463779555777188514)
XLA Ops:
  0.6 0.0 copy-start.3
  0.7 0.7 copy-done.3
  1.3 0.1 copy.12
  1.4 0.1 broadcast_in_dim.12
  1.5 0.1 tile.10
  1.6 0.1 tile.12
  1.7 0.6 pad.4.ct_ref
  2.3 97.7 %shard_map.101 = (bf16[64,16,256]{2,1,0:T(8,128)(2,1)}, f32[4,256,256]{2,1,0:T(8,128)}, f32[4,256,256]{2,1,0:T(8,128)}, f32[2,256]{1,0:T(2,128)}, f32[8,256]{1,0:T(8,128)}) custom-call(bf16[64,16,256]{2,1,0:T(8,128)(2,1)} %x_ref.1, bf16[64,16,256]{2,1,0:T(8,128)(2,1)} %g_ref.1, f32[8,8,128]{2,1,0:T(8,128)} %pad.4.ct_ref, f32[2,256]{1,0:T(2,128)} %gains_ref.1, ...), custom_call_target="tpu_custom_call" | custom-call | tf_op jit(solution)/shard_map/pallas_call | solution.py:734
  100.1 0.0 copy-start.1
  100.1 2.0 %copy.18 = bf16[64,16,256]{2,1,0:T(8,128)(2,1)} copy(bf16[64,16,256]{2,1,0:T(8,128)(2,1)} %get-tuple-element.10) | data formatting | bytes 1048576
  102.0 0.0 copy-done.1
  102.0 0.0 copy-start
  102.0 1.0 copy.19
  103.0 0.6 copy-done
  103.6 0.0 copy-start.4
  103.6 0.0 copy-start.2
  103.6 1.0 copy.20
  104.6 0.0 copy-done.4
  104.6 0.6 copy.21
  105.2 0.0 copy-done.2
  105.2 0.6 copy.22
  (4 shorter events, 0.0 us)
Async XLA Ops:
  0.6 0.7 copy-start.3
  100.1 2.0 %copy-start.1 = (f32[4,256,256]{2,1,0:T(8,128)S(1)}, f32[4,256,256]{2,1,0:T(8,128)}, u32[]{:S(2)}) copy-start(f32[4,256,256]{2,1,0:T(8,128)} %get-tuple-element.11) | copy-start | bytes 3145732
  102.0 1.6 %copy-start = (f32[4,256,256]{2,1,0:T(8,128)S(1)}, f32[4,256,256]{2,1,0:T(8,128)}, u32[]{:S(2)}) copy-start(f32[4,256,256]{2,1,0:T(8,128)} %get-tuple-element.12) | copy-start | bytes 3145732
  103.6 1.0 copy-start.4
  103.6 1.6 %copy-start.2 = (f32[8,256]{1,0:T(8,128)S(1)}, f32[8,256]{1,0:T(8,128)}, u32[]{:S(2)}) copy-start(f32[8,256]{1,0:T(8,128)} %get-tuple-element.14) | copy-start | bytes 24580
